TPU v7x, 512 devices: a whole 4x4x16 slice. The times are simulated.
512 devices in a mesh: ctx: 64 (over y, x, z_lo), head: 8 (over z_hi, core).
Axes of the slice: x: 4, y: 4, z: 16 (z_hi: 4, z_lo: 4; z = z_hi * 4 + z_lo), core: 2. Of those that a mesh axis runs over, the one named last changes fastest.
Arguments:
- x_seq: bfloat16 [16384, 4096], P('ctx', 'head'), may hold values from -0.29882812 to 0.29882812
- grad_out: bfloat16 [16384, 4096], P('ctx', 'head'), may hold values from -0.75 to 0.75
- b_proj: bfloat16 [16384, 128], P('ctx'), may hold values from -0.1796875 to 0.1796875
- c_proj: bfloat16 [16384, 128], P('ctx'), may hold values from -0.1796875 to 0.1796875
- decay_rate: float32 [64, 16384], P('head', 'ctx'), may hold values from 0.4 to 1
Outputs:
- grad_x: bfloat16 [16384, 4096], P('ctx', 'head')
- grad_b: float32 [16384, 128], P(('ctx', 'head'))
- grad_c: float32 [16384, 128], P(('ctx', 'head'))
All inputs are finite; a program needn't handle non-finite values.
Results may differ from a plain program's by a relative error of at most 0.0061.
Values sent between devices are 32-bit elements; how exact they have to be, the bound alone decides.
A program may use at most 128 MiB of HBM per device.

v0:
```python
import jax
import jax.numpy as jnp
from jax import lax
from jax.sharding import PartitionSpec as P

Q = 256


def carried_in(part, axis, combine, identity, reverse):
    count = lax.axis_size(axis)
    place = lax.axis_index(axis)
    ahead = count - 1 - place if reverse else place
    gathered = jax.tree.map(lambda a: lax.all_gather(a, axis), part)
    state = jax.tree.map(lambda a, e: jnp.zeros_like(a) + jnp.asarray(e, a.dtype), part, identity)

    def one(step, state):
        source = count - 1 - step if reverse else step
        return combine(
            state, jax.tree.map(lambda a: lax.dynamic_index_in_dim(a, source, 0, False), gathered)
        )

    return lax.fori_loop(0, ahead, one, state)


def block_weights(cum_block):
    length = cum_block.shape[1]
    later_mask = lax.broadcasted_iota(jnp.int32, (length, length), 0) >= lax.broadcasted_iota(
        jnp.int32, (length, length), 1
    )
    spread = cum_block[:, :, None] - cum_block[:, None, :]
    return jnp.where(later_mask[None], jnp.exp(jnp.where(later_mask[None], spread, 0.0)), 0.0)


def chain_pairs(earlier_pair, later_pair):
    gain_first, state_first = earlier_pair
    gain_second, state_second = later_pair
    return (gain_first * gain_second, gain_second[:, None, None] * state_first + state_second)


def split_heads(rows_blk, head_count):
    return rows_blk.reshape(rows_blk.shape[0], head_count, rows_blk.shape[1] // head_count)


def block_summary(block_args):
    x_blk, dy_blk, b_blk, c_blk, cum_block = block_args
    head_count = cum_block.shape[0]
    x_heads = split_heads(x_blk, head_count)
    dy_heads = split_heads(dy_blk, head_count)
    to_end = jnp.exp(cum_block[:, -1:] - cum_block)
    from_start = jnp.exp(cum_block)
    b_scaled = (b_blk[None] * to_end[:, :, None]).astype(jnp.bfloat16)
    c_scaled = (c_blk[None] * from_start[:, :, None]).astype(jnp.bfloat16)
    local_fwd = jnp.einsum("hsn,shp->hnp", b_scaled, x_heads, preferred_element_type=jnp.float32)
    local_bwd = jnp.einsum("htn,thp->hnp", c_scaled, dy_heads, preferred_element_type=jnp.float32)
    return (jnp.exp(cum_block[:, -1]), local_fwd, local_bwd, b_scaled, to_end, from_start)


def block_local(block_args):
    x_blk, dy_blk, b_blk, c_blk, cum_block = block_args
    head_count = cum_block.shape[0]
    x_heads = split_heads(x_blk, head_count)
    dy_heads = split_heads(dy_blk, head_count)
    weights = block_weights(cum_block)
    inner_prod = jnp.einsum("tn,sn->ts", c_blk, b_blk, preferred_element_type=jnp.float32)
    scores = (inner_prod[None] * weights).astype(jnp.bfloat16)
    pair_dots = jnp.einsum("thp,shp->hts", dy_heads, x_heads, preferred_element_type=jnp.float32)
    pair_weights = (pair_dots * weights).astype(jnp.bfloat16)
    local_x = jnp.einsum("hts,thp->shp", scores, dy_heads, preferred_element_type=jnp.float32)
    local_c = jnp.einsum("hts,sn->tn", pair_weights, b_blk, preferred_element_type=jnp.float32)
    local_b = jnp.einsum("hts,tn->sn", pair_weights, c_blk, preferred_element_type=jnp.float32)
    return (local_x, local_b, local_c)


def block_carried(block_args):
    x_blk, dy_blk, b_scaled, to_end, from_start, entering, leaving = block_args
    head_count = to_end.shape[0]
    x_heads = split_heads(x_blk, head_count)
    dy_heads = split_heads(dy_blk, head_count)
    carried_x = jnp.einsum("hsn,hnp->shp", b_scaled, leaving, preferred_element_type=jnp.float32)
    carried_b = jnp.einsum("shp,hnp->hsn", x_heads, leaving, preferred_element_type=jnp.float32)
    carried_b = jnp.sum(carried_b * to_end[:, :, None], axis=0)
    carried_c = jnp.einsum("thp,hnp->htn", dy_heads, entering, preferred_element_type=jnp.float32)
    carried_c = jnp.sum(carried_c * from_start[:, :, None], axis=0)
    return (carried_x, carried_b, carried_c)


def both_parts(block_args):
    return (block_summary(block_args), block_local(block_args))


def carry_states(block_gain, local_fwd, local_bwd):
    blocks = block_gain.shape[0]
    head_count = block_gain.shape[1]
    total_gain = jnp.ones((head_count,), jnp.float32)
    total_fwd = jnp.zeros_like(local_fwd[0])
    total_bwd = jnp.zeros_like(local_bwd[0])
    position = 0
    total_fwd = block_gain[position][:, None, None] * total_fwd + local_fwd[position]
    total_gain = total_gain * block_gain[position]
    for position in reversed(range(blocks)):
        total_bwd = local_bwd[position] + block_gain[position][:, None, None] * total_bwd
    identity = (jnp.ones((head_count,), jnp.float32), jnp.zeros_like(total_fwd))
    arriving_gain, arriving = carried_in(
        (total_gain, total_fwd), "ctx", chain_pairs, identity, False
    )
    returning_gain, returning = carried_in(
        (total_gain, total_bwd), "ctx", chain_pairs, identity, True
    )
    carried_state = arriving
    position = 0
    entering_list = [carried_state.astype(jnp.bfloat16)]
    leaving_list = []
    carried_state = returning
    for position in reversed(range(blocks)):
        leaving_list.insert(0, carried_state.astype(jnp.bfloat16))
        carried_state = local_bwd[position] + block_gain[position][:, None, None] * carried_state
    return (jnp.stack(entering_list), jnp.stack(leaving_list))


def on_device(x_seq, grad_out, b_proj, c_proj, decay_rate):
    tokens = x_seq.shape[0]
    head_count = decay_rate.shape[0]
    blocks = tokens // Q
    cum_log = jnp.cumsum(jnp.log(decay_rate).reshape(head_count, blocks, Q), axis=2)
    cum_log = jnp.transpose(cum_log, (1, 0, 2))
    x_blocks = x_seq.reshape(blocks, Q, x_seq.shape[1])
    dy_blocks = grad_out.reshape(blocks, Q, grad_out.shape[1])
    b_blocks = b_proj.reshape(blocks, Q, b_proj.shape[1])
    c_blocks = c_proj.reshape(blocks, Q, c_proj.shape[1])
    inputs = (x_blocks, dy_blocks, b_blocks, c_blocks, cum_log)
    summaries, local_terms = lax.map(both_parts, inputs)
    block_gain, local_fwd, local_bwd, b_scaled, to_end, from_start = summaries
    entering, leaving = carry_states(block_gain, local_fwd, local_bwd)
    local_x, local_b, local_c = local_terms
    local_b = local_b.reshape(tokens, local_b.shape[2])
    local_c = local_c.reshape(tokens, local_c.shape[2])
    carried_x, carried_b, carried_c = lax.map(
        block_carried, (x_blocks, dy_blocks, b_scaled, to_end, from_start, entering, leaving)
    )
    carried_b = carried_b.reshape(tokens, carried_b.shape[2])
    carried_c = carried_c.reshape(tokens, carried_c.shape[2])
    grad_x = (local_x + carried_x).astype(jnp.bfloat16).reshape(tokens, x_seq.shape[1])
    grad_b, grad_c = (
        lax.psum_scatter(local_b + carried_b, "head", scatter_dimension=0, tiled=True),
        lax.psum_scatter(local_c + carried_c, "head", scatter_dimension=0, tiled=True),
    )
    return (grad_x, grad_b, grad_c)


def solution(mesh):
    placed = (P("ctx", "head"), P("ctx", "head"), P("ctx", None), P("ctx", None), P("head", "ctx"))
    return jax.shard_map(
        on_device,
        mesh=mesh,
        in_specs=placed,
        out_specs=(P("ctx", "head"), P(("ctx", "head"), None), P(("ctx", "head"), None)),
        check_vma=False,
    )
```

profile of v0, /device:TPU:1, one launch (start us, length us, event | category | flops | bytes accessed | tf_op | source)
XLA Modules:
  0.0 1000.7 jit_solution(11440587366166055512)
XLA Ops:
  9.1 1.1 copy.47
  11.0 1.2 convolution_add_fusion.1
  13.4 1.2 convolution_add_fusion
  14.7 1.4 dynamic-slice.9
  17.0 170.7 %all-reduce = f32[512]{0:T(512)S(1)} all-reduce(f32[512]{0:T(512)S(1)} %dynamic-update-slice), channel_id=2, replica_groups=mesh['ctx'=64,'head'=8] {'ctx'}, use_global_device_ids=true, to_apply=%add | all-reduce | flops 512 | bytes 4096
  188.8 213.5 %all-gather.6.cloned.1.call-done = f32[512,128,64]{1,2,0:T(8,128)} async-done(((f32[8,128,64]{1,2,0:T(8,128)}), f32[512,128,64]{1,2,0:T(8,128)}) %all-gather.6.cloned.1.call-update) | async-done | bytes 16777232 | tf_op jit(solution)/shard_map/all_gather | solution.py:13
  402.4 86.5 %while.16 = (s32[]{:T(128)}, f32[8,128,64]{2,1,0:T(8,128)S(1)}, s32[]{:T(128)}, f32[64,8]{1,0:T(8,128)S(1)}, f32[64,8,128,64]{2,3,1,0:T(8,128)}, /*index=5*/s32[]{:T(128)}, s32[]{:T(128)}, s32[]{:T(128)}, s32[]{:T(128)}) while((s32[]{:T(128)}, f32[8,128,64]{2,1,0:T(8,128)S(1)}, s32[]{:T(128)}, f32[64,8]{1,0:T(8,128)S(1)}, ...), condition=%wide.region_3.4_spmd, body=%wide.region_2.3_spmd.sunk | while | flops 131078 | bytes 1835259 | solution.py:22
  402.4 1.0 constant_dynamic-slice_fusion.4
  403.8 1.0 constant_dynamic-slice_fusion.4
  405.2 1.0 constant_dynamic-slice_fusion.4
  406.5 1.0 constant_dynamic-slice_fusion.4
  407.9 1.0 constant_dynamic-slice_fusion.4
  409.3 1.0 constant_dynamic-slice_fusion.4
  410.6 1.0 constant_dynamic-slice_fusion.4
  412.0 1.0 constant_dynamic-slice_fusion.4
  413.4 1.0 constant_dynamic-slice_fusion.4
  414.8 1.0 constant_dynamic-slice_fusion.4
  416.1 1.0 constant_dynamic-slice_fusion.4
  417.5 1.0 constant_dynamic-slice_fusion.4
  418.9 1.0 constant_dynamic-slice_fusion.4
  420.2 1.0 constant_dynamic-slice_fusion.4
  421.6 1.0 constant_dynamic-slice_fusion.4
  423.0 1.0 constant_dynamic-slice_fusion.4
  424.4 1.0 constant_dynamic-slice_fusion.4
  425.7 1.0 constant_dynamic-slice_fusion.4
  427.1 1.0 constant_dynamic-slice_fusion.4
  428.5 1.0 constant_dynamic-slice_fusion.4
  429.8 1.0 constant_dynamic-slice_fusion.4
  431.2 1.0 constant_dynamic-slice_fusion.4
  432.6 1.0 constant_dynamic-slice_fusion.4
  434.0 1.0 constant_dynamic-slice_fusion.4
  435.3 1.0 constant_dynamic-slice_fusion.4
  436.7 1.0 constant_dynamic-slice_fusion.4
  438.1 1.0 constant_dynamic-slice_fusion.4
  439.4 1.0 constant_dynamic-slice_fusion.4
  440.8 1.0 constant_dynamic-slice_fusion.4
  442.2 1.0 constant_dynamic-slice_fusion.4
  443.6 1.0 constant_dynamic-slice_fusion.4
  444.9 1.0 constant_dynamic-slice_fusion.4
  446.3 1.0 constant_dynamic-slice_fusion.4
  447.7 1.0 constant_dynamic-slice_fusion.4
  449.0 1.0 constant_dynamic-slice_fusion.4
  450.4 1.0 constant_dynamic-slice_fusion.4
  451.8 1.0 constant_dynamic-slice_fusion.4
  453.2 1.0 constant_dynamic-slice_fusion.4
  454.5 1.0 constant_dynamic-slice_fusion.4
  455.9 1.0 constant_dynamic-slice_fusion.4
  457.3 1.0 constant_dynamic-slice_fusion.4
  458.7 1.0 constant_dynamic-slice_fusion.4
  460.0 1.0 constant_dynamic-slice_fusion.4
  461.4 1.0 constant_dynamic-slice_fusion.4
  462.8 1.0 constant_dynamic-slice_fusion.4
  464.2 1.0 constant_dynamic-slice_fusion.4
  465.5 1.0 constant_dynamic-slice_fusion.4
  466.9 1.0 constant_dynamic-slice_fusion.4
  477.9 1.0 constant_dynamic-slice_fusion.4
  479.2 1.0 constant_dynamic-slice_fusion.4
  483.4 1.0 constant_dynamic-slice_fusion.4
  484.7 1.0 constant_dynamic-slice_fusion.4
  486.1 1.0 constant_dynamic-slice_fusion.4
  487.5 1.0 constant_dynamic-slice_fusion.4
  490.2 331.5 %all-gather.8.cloned.1.call-done = f32[512,128,64]{1,2,0:T(8,128)} async-done(((f32[8,128,64]{1,2,0:T(8,128)}), f32[512,128,64]{1,2,0:T(8,128)}) %all-gather.8.cloned.1.call-update) | async-done | bytes 16777232 | tf_op jit(solution)/shard_map/all_gather | solution.py:13
  825.1 84.7 %reduce-scatter.3.cloned.1.call-done = f32[32,128]{1,0:T(8,128)} async-done(((f32[256,128]{1,0:T(8,128)}), f32[32,128]{1,0:T(8,128)}) %reduce-scatter.3.cloned.1.call-update) | async-done | bytes 16400 | tf_op jit(solution)/shard_map/reduce_scatter | solution.py:144
  909.8 84.4 %reduce-scatter.5.cloned.1.call-done = f32[32,128]{1,0:T(8,128)} async-done(((f32[256,128]{1,0:T(8,128)}), f32[32,128]{1,0:T(8,128)}) %reduce-scatter.5.cloned.1.call-update) | async-done | bytes 16400 | tf_op jit(solution)/shard_map/reduce_scatter | solution.py:145
  (242 shorter events, 41.1 us)
Async XLA Ops:
  7.2 180.7 %copy-start = (bf16[256,128]{1,0:T(8,128)(2,1)S(1)}, bf16[256,128]{1,0:T(8,128)(2,1)}, u32[]{:S(2)}) copy-start(bf16[256,128]{1,0:T(8,128)(2,1)} %param.12) | copy-start | bytes 196612
  7.2 180.7 %copy-start.1 = (bf16[256,128]{1,0:T(8,128)(2,1)S(1)}, bf16[256,128]{1,0:T(8,128)(2,1)}, u32[]{:S(2)}) copy-start(bf16[256,128]{1,0:T(8,128)(2,1)} %param.11) | copy-start | bytes 196612
  7.2 6.0 copy-start.2
  7.2 395.1 %all-gather.6.cloned.1.call-start = ((), (), s32[]{:S(2)}) async-start(), calls=%async_computation.4 | async-start | bytes 17039360 | tf_op jit(solution)/shard_map/all_gather | solution.py:13
  12.2 809.4 %all-gather.8.cloned.1.call-start = ((), (), s32[]{:S(2)}) async-start(), calls=%async_computation.5 | async-start | bytes 17039360 | tf_op jit(solution)/shard_map/all_gather | solution.py:13
  14.6 895.2 %reduce-scatter.3.cloned.1.call-start = ((), (), s32[]{:S(2)}) async-start(), calls=%async_computation.2 | async-start | bytes 147456 | tf_op jit(solution)/shard_map/reduce_scatter | solution.py:144
  490.1 504.1 %reduce-scatter.5.cloned.1.call-start = ((), (), s32[]{:S(2)}) async-start(), calls=%async_computation.3 | async-start | bytes 147456 | tf_op jit(solution)/shard_map/reduce_scatter | solution.py:145
Sparse Core Ops, SparseCore 0:
  12.4 389.9 all-gather.5
  404.4 417.1 all-gather.7
  825.0 84.7 reduce-scatter.2
  913.2 80.9 reduce-scatter.4
where the time goes:
time: 1000 us
  waiting for transfers between devices  714 us (71%)
  blocking collectives  171 us (17%)
  local copies, waits for them, and re-layouts  79.8 us (8%)
  between operations  14.6 us (1%)
  other arithmetic  11.5 us (1%)
    all_gather x2, waiting for transfers between devices, carried_in(): gathered = jax.tree.map(lambda a: lax.all_gather(a, axis), part)  545 us
    unnamed x1, blocking collectives  171 us
    reduce_scatter x1, waiting for transfers between devices, on_device(): lax.psum_scatter(local_b + carried_b, 'head', scatter_dimension=0, tiled=...  84.7 us
    reduce_scatter x1, waiting for transfers between devices, on_device(): lax.psum_scatter(local_c + carried_c, 'head', scatter_dimension=0, tiled=...  84.4 us
    dynamic_slice x126, local copies, waits for them, and re-layouts, one(): lax.dynamic_index_in_dim(a, source, 0, False)  74 us
  transfers between devices with their start and end apart: 4, of which 4 were waited for; matrix products, arithmetic and copies ran while one was open for 9% of the time, Pallas kernels for 0%

commit v1 on v0

v1 whole, which is shorter than its diff:
```python
import jax
import jax.numpy as jnp
from jax import lax
from jax.experimental import pallas as pl
from jax.experimental.pallas import tpu as pltpu
from jax.sharding import PartitionSpec as P

MESH = pl.DeviceIdType.MESH
Q = 256
HEADS = 8
WIDTH = 64
STATE = 128
BLOCKS = 4
GROUP = 32
ROWS = 16
LINES = 16
PART = 32

NN = (((1,), (0,)), ((), ()))
NT = (((1,), (1,)), ((), ()))
TN = (((0,), (0,)), ((), ()))


def dot(a, b, dims):
    return lax.dot_general(a, b, dims, preferred_element_type=jnp.float32)


def kernel(
    x_ref, dy_ref, b_ref, c_ref, decay_ref,
    gx_ref, gb_ref, gc_ref,
    fwd_out, bwd_out, gain_out, fwd_in, bwd_in, gain_in,
    fwd_tot, bwd_tot, gain_tot, fwd_oth, bwd_oth, gain_oth,
    enter_out, leave_out, enter_in, leave_in,
    xs_ref, ys_ref, end_ref, local_x, local_b, local_c,
    core_out, core_in, part_out, part_in,
    send_sems, recv_sems,
):
    me = lax.axis_index("ctx")
    head = lax.axis_index("head")
    line = me // 4
    half = (me // 2) % 2
    mine = line * 2 + me % 2
    core = head % 2
    z_hi = head // 2

    def ctx_of(i):
        return (i // 2) * 4 + half * 2 + i % 2

    other_half = {"ctx": line * 4 + (1 - half) * 2 + me % 2}
    other_core = {"head": z_hi * 2 + 1 - core}

    barrier = pltpu.get_barrier_semaphore()

    def greet(k, carry):
        pl.semaphore_signal(
            barrier, inc=1, device_id={"ctx": ctx_of(lax.rem(mine + k, GROUP))}, device_id_type=MESH
        )
        return carry

    lax.fori_loop(1, GROUP, greet, 0)
    pl.semaphore_signal(barrier, inc=1, device_id=other_half, device_id_type=MESH)
    pl.semaphore_signal(barrier, inc=1, device_id=other_core, device_id_type=MESH)
    for k in range(1, 4):
        pl.semaphore_signal(
            barrier, inc=1, device_id={"head": lax.rem(head + 2 * k, 8)}, device_id_type=MESH
        )

    lane = lax.broadcasted_iota(jnp.int32, (HEADS, Q), 1)
    cum = jnp.log(decay_ref[...])
    step = 1
    while step < Q:
        cum = cum + jnp.where(lane >= step, pltpu.roll(cum, step, 1), 0.0)
        step *= 2
    to_end = jnp.exp(cum[:, Q - 1 : Q] - cum)
    from_start = jnp.exp(cum)
    columns = jnp.transpose(jnp.concatenate([cum, to_end, from_start], axis=0))
    first_lanes = lax.broadcasted_iota(jnp.int32, (Q, 128), 1) < WIDTH
    b_blk = b_ref[...]
    c_blk = c_ref[...]

    def spread(base, block):
        left = jnp.broadcast_to(columns[:, base + 2 * block : base + 2 * block + 1], (Q, 128))
        right = jnp.broadcast_to(columns[:, base + 2 * block + 1 : base + 2 * block + 2], (Q, 128))
        return jnp.where(first_lanes, left, right)

    for block in range(BLOCKS):
        at = slice(block * 128, block * 128 + 128)
        end_blk = spread(HEADS, block)
        start_blk = spread(2 * HEADS, block)
        end_ref[:, at] = end_blk
        xs = (x_ref[:, at].astype(jnp.float32) * end_blk).astype(jnp.bfloat16)
        ys = (dy_ref[:, at].astype(jnp.float32) * start_blk).astype(jnp.bfloat16)
        xs_ref[:, at] = xs
        ys_ref[:, at] = ys
        gain_out[block] = start_blk[Q - 1 : Q, :]
        bwd_out[block * 8 : block * 8 + 8] = dot(c_blk, ys, TN).reshape(8, ROWS, 128)
        fwd_out[block * 8 : block * 8 + 8] = dot(b_blk, xs, TN).reshape(8, ROWS, 128)

    pl.semaphore_wait(barrier, GROUP - 1 + 1 + 1 + 3)

    def scatter(out, into, n):
        def one(k, carry):
            i = lax.rem(mine + k, GROUP)
            pltpu.make_async_remote_copy(
                src_ref=out.at[i], dst_ref=into.at[mine], send_sem=send_sems.at[n],
                recv_sem=recv_sems.at[n], device_id={"ctx": ctx_of(i)}, device_id_type=MESH,
            ).start()
            return carry

        lax.fori_loop(1, GROUP, one, 0)

    def send_gains(k, carry):
        i = lax.rem(mine + k, GROUP)
        pltpu.make_async_remote_copy(
            src_ref=gain_out.at[i // 8], dst_ref=gain_in.at[mine], send_sem=send_sems.at[0],
            recv_sem=recv_sems.at[0], device_id={"ctx": ctx_of(i)}, device_id_type=MESH,
        ).start()
        return carry

    def wait_bytes(ref, sems, n):
        pltpu.make_async_copy(ref, ref, sems.at[n]).wait()

    lax.fori_loop(1, GROUP, send_gains, 0)
    scatter(bwd_out, bwd_in, 1)
    scatter(fwd_out, fwd_in, 2)
    gain_in[mine] = gain_out[mine // 8]
    bwd_in[mine] = bwd_out[mine]
    fwd_in[mine] = fwd_out[mine]

    row = lax.broadcasted_iota(jnp.int32, (Q, Q), 0)
    col = lax.broadcasted_iota(jnp.int32, (Q, Q), 1)
    later = col >= row
    inner = dot(b_blk, c_blk, NT)
    pairs = jnp.zeros((Q, Q), jnp.float32)
    for block in range(BLOCKS):
        at = slice(block * 128, block * 128 + 128)
        x_blk = x_ref[:, at]
        dy_blk = dy_ref[:, at]
        parts = []
        for side in range(2):
            h = 2 * block + side
            diff = cum[h : h + 1, :] - columns[:, h : h + 1]
            weights = jnp.exp(jnp.where(later, diff, -1e30))
            x_side = jnp.where(first_lanes == (side == 0), x_blk, jnp.zeros_like(x_blk))
            pairs = pairs + dot(x_side, dy_blk, NT) * weights
            scores = (inner * weights).astype(jnp.bfloat16)
            parts.append(dot(scores, dy_blk, NN))
        local_x[:, at] = jnp.where(first_lanes, parts[0], parts[1])
    local_b[...] = dot(pairs.astype(jnp.bfloat16), c_blk, NN)
    local_c[...] = dot(jnp.transpose(pairs).astype(jnp.bfloat16), b_blk, NN)

    def exchange(src, dst, n):
        copy = pltpu.make_async_remote_copy(
            src_ref=src, dst_ref=dst, send_sem=send_sems.at[n], recv_sem=recv_sems.at[n],
            device_id=other_half, device_id_type=MESH,
        )
        copy.start()
        return copy

    wait_bytes(gain_in.at[pl.ds(0, GROUP - 1)], recv_sems, 0)
    wait_bytes(bwd_in.at[pl.ds(0, GROUP - 1)], recv_sems, 1)
    for l in range(LINES):
        gain_tot[l] = gain_in[2 * l] * gain_in[2 * l + 1]
        bwd_tot[l] = bwd_in[2 * l] + gain_in[2 * l] * bwd_in[2 * l + 1]
    gain_copy = exchange(gain_tot, gain_oth, 3)
    bwd_copy = exchange(bwd_tot, bwd_oth, 4)
    wait_bytes(fwd_in.at[pl.ds(0, GROUP - 1)], recv_sems, 2)
    for l in range(LINES):
        fwd_tot[l] = fwd_in[2 * l] * gain_in[2 * l + 1] + fwd_in[2 * l + 1]
    fwd_copy = exchange(fwd_tot, fwd_oth, 5)

    is_left = jnp.full((ROWS, 128), half) == 0

    gain_copy.wait()
    bwd_copy.wait()
    cur = jnp.zeros((ROWS, 128), jnp.float32)
    for l in reversed(range(LINES)):
        cur = jnp.where(is_left, bwd_oth[l] + gain_oth[l] * cur, cur)
        leave_out[2 * l + 1] = cur
        cur = bwd_in[2 * l + 1] + gain_in[2 * l + 1] * cur
        leave_out[2 * l] = cur
        cur = bwd_in[2 * l] + gain_in[2 * l] * cur
        cur = jnp.where(is_left, cur, bwd_oth[l] + gain_oth[l] * cur)
    scatter(leave_out, leave_in, 6)
    leave_in[mine] = leave_out[mine]

    fwd_copy.wait()
    cur = jnp.zeros((ROWS, 128), jnp.float32)
    for l in range(LINES):
        cur = jnp.where(is_left, cur, fwd_oth[l] + gain_oth[l] * cur)
        enter_out[2 * l] = cur
        cur = fwd_in[2 * l] + gain_in[2 * l] * cur
        enter_out[2 * l + 1] = cur
        cur = fwd_in[2 * l + 1] + gain_in[2 * l + 1] * cur
        cur = jnp.where(is_left, fwd_oth[l] + gain_oth[l] * cur, cur)
    scatter(enter_out, enter_in, 7)
    enter_in[mine] = enter_out[mine]

    wait_bytes(leave_in.at[pl.ds(0, GROUP - 1)], recv_sems, 6)
    sum_b = local_b[...]
    for block in range(BLOCKS):
        at = slice(block * 128, block * 128 + 128)
        leave = leave_in[block * 8 : block * 8 + 8].reshape(STATE, 128).astype(jnp.bfloat16)
        gx_ref[:, at] = (local_x[:, at] + end_ref[:, at] * dot(b_blk, leave, NN)).astype(jnp.bfloat16)
        sum_b = sum_b + dot(xs_ref[:, at], leave, NT)
    core_out[:, :, 0] = sum_b.reshape(4, 2, PART, 128)

    wait_bytes(enter_in.at[pl.ds(0, GROUP - 1)], recv_sems, 7)
    sum_c = local_c[...]
    for block in range(BLOCKS):
        at = slice(block * 128, block * 128 + 128)
        enter = enter_in[block * 8 : block * 8 + 8].reshape(STATE, 128).astype(jnp.bfloat16)
        sum_c = sum_c + dot(ys_ref[:, at], enter, NT)
    core_out[:, :, 1] = sum_c.reshape(4, 2, PART, 128)

    core_copy = pltpu.make_async_remote_copy(
        src_ref=core_out.at[:, 1 - core], dst_ref=core_in, send_sem=send_sems.at[8],
        recv_sem=recv_sems.at[8], device_id=other_core, device_id_type=MESH,
    )
    core_copy.start()
    core_copy.wait()
    part_out[...] = core_out[:, core] + core_in[...]
    copies = []
    for k in (2, 1, 3):
        to = lax.rem(z_hi + k, 4)
        copy = pltpu.make_async_remote_copy(
            src_ref=part_out.at[to], dst_ref=part_in.at[k - 1], send_sem=send_sems.at[8 + k],
            recv_sem=recv_sems.at[8 + k], device_id={"head": to * 2 + core}, device_id_type=MESH,
        )
        copy.start()
        copies.append(copy)
    for copy in copies:
        copy.wait()
    total = part_out[z_hi] + part_in[0] + part_in[1] + part_in[2]
    gb_ref[...] = total[0]
    gc_ref[...] = total[1]

    wait_bytes(gain_in.at[pl.ds(0, GROUP - 1)], send_sems, 0)
    for n, ref in ((1, bwd_in), (2, fwd_in), (6, leave_in), (7, enter_in)):
        wait_bytes(ref.at[pl.ds(0, GROUP - 1)], send_sems, n)


def on_device(x_seq, grad_out, b_proj, c_proj, decay_rate):
    def vmem(shape, dtype=jnp.float32):
        return pltpu.VMEM(shape, dtype)

    chunks = (GROUP, ROWS, 128)
    totals = (LINES, ROWS, 128)
    return pl.pallas_call(
        kernel,
        out_shape=(
            jax.ShapeDtypeStruct((Q, HEADS * WIDTH), jnp.bfloat16),
            jax.ShapeDtypeStruct((PART, STATE), jnp.float32),
            jax.ShapeDtypeStruct((PART, STATE), jnp.float32),
        ),
        in_specs=[pl.BlockSpec(memory_space=pltpu.VMEM)] * 5,
        out_specs=(pl.BlockSpec(memory_space=pltpu.VMEM),) * 3,
        scratch_shapes=[
            vmem(chunks), vmem(chunks), vmem((BLOCKS, 1, 128)),
            vmem(chunks), vmem(chunks), vmem((GROUP, 1, 128)),
            vmem(totals), vmem(totals), vmem((LINES, 1, 128)),
            vmem(totals), vmem(totals), vmem((LINES, 1, 128)),
            vmem(chunks), vmem(chunks), vmem(chunks), vmem(chunks),
            vmem((Q, HEADS * WIDTH), jnp.bfloat16), vmem((Q, HEADS * WIDTH), jnp.bfloat16),
            vmem((Q, HEADS * WIDTH)), vmem((Q, HEADS * WIDTH)),
            vmem((Q, STATE)), vmem((Q, STATE)),
            vmem((4, 2, 2, PART, 128)), vmem((4, 2, PART, 128)),
            vmem((4, 2, PART, 128)), vmem((3, 2, PART, 128)),
            pltpu.SemaphoreType.DMA((12,)), pltpu.SemaphoreType.DMA((12,)),
        ],
        compiler_params=pltpu.CompilerParams(
            collective_id=0, has_side_effects=True, vmem_limit_bytes=40 << 20
        ),
    )(x_seq, grad_out, b_proj, c_proj, decay_rate)


def solution(mesh):
    placed = (P("ctx", "head"), P("ctx", "head"), P("ctx", None), P("ctx", None), P("head", "ctx"))
    return jax.shard_map(
        on_device,
        mesh=mesh,
        in_specs=placed,
        out_specs=(P("ctx", "head"), P(("ctx", "head"), None), P(("ctx", "head"), None)),
        check_vma=False,
    )
```

time: 1000 us -> 59.9 us (0.06)
  the two profiles are of different devices: /device:TPU:1 before, /device:TPU:32 now
where the time goes in v1:
time: 59.9 us; the launch traced here: 59.6 us
  Pallas kernels  52.8 us (88%)
  local copies, waits for them, and re-layouts  6.18 us (10%)
  between operations  0.65 us (1%)
    pallas_call x1, Pallas kernels, on_device(): pl.pallas_call(kernel, out_shape=(jax.ShapeDtypeStruct((Q, HEADS * WIDTH)...  52.8 us
    unnamed x13, local copies, waits for them, and re-layouts  6.18 us

profile of v1, /device:TPU:32, one launch (start us, length us, event | category | flops | bytes accessed | tf_op | source)
XLA Modules:
  0.0 59.6 jit_solution(6878904466056246153)
XLA Ops:
  0.6 0.0 copy-start
  0.6 0.9 %copy-done = bf16[256,512]{1,0:T(8,128)(2,1)S(1)} copy-done((bf16[256,512]{1,0:T(8,128)(2,1)S(1)}, bf16[256,512]{1,0:T(8,128)(2,1)}, u32[]{:S(2)}) %copy-start) | copy-done | bytes 262168
  1.6 0.0 copy-start.1
  1.6 0.9 %copy-done.1 = bf16[256,512]{1,0:T(8,128)(2,1)S(1)} copy-done((bf16[256,512]{1,0:T(8,128)(2,1)S(1)}, bf16[256,512]{1,0:T(8,128)(2,1)}, u32[]{:S(2)}) %copy-start.1) | copy-done | bytes 262168
  2.5 0.0 copy-start.2
  2.5 0.8 %copy-done.2 = bf16[256,128]{1,0:T(8,128)(2,1)S(1)} copy-done((bf16[256,128]{1,0:T(8,128)(2,1)S(1)}, bf16[256,128]{1,0:T(8,128)(2,1)}, u32[]{:S(2)}) %copy-start.2) | copy-done | bytes 65560
  3.4 0.0 copy-start.3
  3.4 0.8 %copy-done.3 = bf16[256,128]{1,0:T(8,128)(2,1)S(1)} copy-done((bf16[256,128]{1,0:T(8,128)(2,1)S(1)}, bf16[256,128]{1,0:T(8,128)(2,1)}, u32[]{:S(2)}) %copy-start.3) | copy-done | bytes 65560
  4.2 0.0 copy-start.4
  4.2 0.7 %copy-done.4 = f32[8,256]{1,0:T(8,128)S(1)} copy-done((f32[8,256]{1,0:T(8,128)S(1)}, f32[8,256]{1,0:T(8,128)}, u32[]{:S(2)}) %copy-start.4) | copy-done | bytes 8216
  4.9 52.8 %shard_map.76 = (bf16[256,512]{1,0:T(8,128)(2,1)S(1)}, f32[32,128]{1,0:T(8,128)S(1)}, f32[32,128]{1,0:T(8,128)S(1)}) custom-call(bf16[256,512]{1,0:T(8,128)(2,1)S(1)} %copy-done, bf16[256,512]{1,0:T(8,128)(2,1)S(1)} %copy-done.1, bf16[256,128]{1,0:T(8,128)(2,1)S(1)} %copy-done.2, bf16[256,128]{1,0:T(8,128)(2,1)S(1)} %copy-done.3, f32[8,256]{1,0:T(8,128)S(1)} %copy-done.4), custom_call_target="tpu_custom_call" | custom-call | tf_op jit(solution)/shard_map/pallas_call | solution.py:249
  57.7 0.7 %copy.11 = bf16[256,512]{1,0:T(8,128)(2,1)} copy(bf16[256,512]{1,0:T(8,128)(2,1)S(1)} %get-tuple-element.6) | data formatting | bytes 524288
  58.4 0.6 %copy.12 = f32[32,128]{1,0:T(8,128)} copy(f32[32,128]{1,0:T(8,128)S(1)} %get-tuple-element.7) | data formatting | bytes 32768
  59.0 0.6 %copy.13 = f32[32,128]{1,0:T(8,128)} copy(f32[32,128]{1,0:T(8,128)S(1)} %get-tuple-element.8) | data formatting | bytes 32768
Async XLA Ops:
  0.6 1.0 %copy-start = (bf16[256,512]{1,0:T(8,128)(2,1)S(1)}, bf16[256,512]{1,0:T(8,128)(2,1)}, u32[]{:S(2)}) copy-start(bf16[256,512]{1,0:T(8,128)(2,1)} %x_ref.1) | copy-start | bytes 786436
  1.6 0.9 %copy-start.1 = (bf16[256,512]{1,0:T(8,128)(2,1)S(1)}, bf16[256,512]{1,0:T(8,128)(2,1)}, u32[]{:S(2)}) copy-start(bf16[256,512]{1,0:T(8,128)(2,1)} %dy_ref.1) | copy-start | bytes 786436
  2.5 0.8 %copy-start.2 = (bf16[256,128]{1,0:T(8,128)(2,1)S(1)}, bf16[256,128]{1,0:T(8,128)(2,1)}, u32[]{:S(2)}) copy-start(bf16[256,128]{1,0:T(8,128)(2,1)} %b_ref.1) | copy-start | bytes 196612
  3.4 0.8 %copy-start.3 = (bf16[256,128]{1,0:T(8,128)(2,1)S(1)}, bf16[256,128]{1,0:T(8,128)(2,1)}, u32[]{:S(2)}) copy-start(bf16[256,128]{1,0:T(8,128)(2,1)} %c_ref.1) | copy-start | bytes 196612
  4.2 0.7 %copy-start.4 = (f32[8,256]{1,0:T(8,128)S(1)}, f32[8,256]{1,0:T(8,128)}, u32[]{:S(2)}) copy-start(f32[8,256]{1,0:T(8,128)} %decay_ref.1) | copy-start | bytes 24580

commit v2 on v1

v2 whole, which is shorter than its diff:
```python
import jax
import jax.numpy as jnp
from jax import lax
from jax.experimental import pallas as pl
from jax.experimental.pallas import tpu as pltpu
from jax.sharding import PartitionSpec as P

MESH = pl.DeviceIdType.MESH
Q = 256
HEADS = 8
WIDTH = 64
STATE = 128
BLOCKS = 4
GROUP = 32
ROWS = 16
LINES = 16
PART = 32
PIECES = 4

NN = (((1,), (0,)), ((), ()))
NT = (((1,), (1,)), ((), ()))
TN = (((0,), (0,)), ((), ()))


def dot(a, b, dims):
    return lax.dot_general(a, b, dims, preferred_element_type=jnp.float32)


def kernel(
    x_hbm, dy_hbm, b_hbm, c_hbm, decay_hbm,
    gx_hbm, gb_hbm, gc_hbm,
    x_ref, dy_ref, b_ref, c_ref, decay_ref, gx_ref, gb_ref, gc_ref,
    fwd_out, bwd_out, gain_out, fwd_in, bwd_in, gain_in,
    fwd_tot, bwd_tot, gain_tot, fwd_oth, bwd_oth, gain_oth,
    enter_out, leave_out, enter_in, leave_in,
    xs_ref, ys_ref, end_ref, local_x, local_b, local_c,
    core_out, core_in, part_out, part_in,
    in_sems, send_sems, recv_sems, fwd_sems, bwd_sems, mid_fwd_sems, mid_bwd_sems, mid_gain_sems,
    gain_sems, core_sems, part_send, part_recv, out_sems, ready,
):
    me = lax.axis_index("ctx")
    head = lax.axis_index("head")
    line = me // 4
    plane_of_me = me // 16
    half = (me // 2) % 2
    mine = line * 2 + me % 2
    core = head % 2
    z_hi = head // 2

    def ctx_of(i):
        return (i // 2) * 4 + half * 2 + i % 2

    other_half = {"ctx": line * 4 + (1 - half) * 2 + me % 2}
    other_core = {"head": z_hi * 2 + 1 - core}
    early = z_hi == 0

    loads = []
    for n, (src, dst) in enumerate((
        (decay_hbm, decay_ref), (c_hbm, c_ref), (b_hbm, b_ref), (dy_hbm, dy_ref), (x_hbm, x_ref)
    )):
        loads.append(pltpu.make_async_copy(src, dst, in_sems.at[n]))
        loads[-1].start()

    barrier = pltpu.get_barrier_semaphore()

    def greet(k, carry):
        pl.semaphore_signal(
            barrier, inc=1, device_id={"ctx": ctx_of(lax.rem(mine + k, GROUP))}, device_id_type=MESH
        )
        return carry

    lax.fori_loop(1, GROUP, greet, 0)
    pl.semaphore_signal(barrier, inc=1, device_id=other_half, device_id_type=MESH)
    pl.semaphore_signal(barrier, inc=1, device_id=other_core, device_id_type=MESH)
    def tell_later(sem):
        for k in range(1, 4):
            pl.semaphore_signal(sem, inc=1, device_id={"head": k * 2 + core}, device_id_type=MESH)

    @pl.when(early)
    def _():
        tell_later(barrier)

    loads[0].wait()
    lane = lax.broadcasted_iota(jnp.int32, (HEADS, Q), 1)
    cum = jnp.log(decay_ref[...])
    step = 1
    while step < Q:
        cum = cum + jnp.where(lane >= step, pltpu.roll(cum, step, 1), 0.0)
        step *= 2
    to_end = jnp.exp(cum[:, Q - 1 : Q] - cum)
    from_start = jnp.exp(cum)
    columns = jnp.transpose(jnp.concatenate([cum, to_end, from_start], axis=0))
    first_lanes = lax.broadcasted_iota(jnp.int32, (Q, 128), 1) < WIDTH
    for load in loads[1:]:
        load.wait()
    b_blk = b_ref[...]
    c_blk = c_ref[...]

    def spread(base, block):
        left = jnp.broadcast_to(columns[:, base + 2 * block : base + 2 * block + 1], (Q, 128))
        right = jnp.broadcast_to(columns[:, base + 2 * block + 1 : base + 2 * block + 2], (Q, 128))
        return jnp.where(first_lanes, left, right)

    for block in range(BLOCKS):
        at = slice(block * 128, block * 128 + 128)
        end_blk = spread(HEADS, block)
        start_blk = spread(2 * HEADS, block)
        end_ref[:, at] = end_blk
        xs = (x_ref[:, at].astype(jnp.float32) * end_blk).astype(jnp.bfloat16)
        ys = (dy_ref[:, at].astype(jnp.float32) * start_blk).astype(jnp.bfloat16)
        xs_ref[:, at] = xs
        ys_ref[:, at] = ys
        gain_out[block] = start_blk[Q - 1 : Q, :]
        bwd_out[block * 8 : block * 8 + 8] = dot(c_blk, ys, TN).reshape(8, ROWS, 128)
        fwd_out[block * 8 : block * 8 + 8] = dot(b_blk, xs, TN).reshape(8, ROWS, 128)

    pl.semaphore_wait(barrier, GROUP - 1 + 1 + 1 + jnp.where(early, 0, 1))

    def send_to(i, src, dst, send_sem, recv_sem):
        pltpu.make_async_remote_copy(
            src_ref=src, dst_ref=dst, send_sem=send_sem, recv_sem=recv_sem,
            device_id={"ctx": ctx_of(i)}, device_id_type=MESH,
        ).start()

    def scatter(out_of, into, send_sem, recv_sem):
        for k in (0, 1, 3, 2):
            first = lax.rem(plane_of_me + k, 4) * 8

            def one(j, carry, first=first):
                i = first + lax.rem(mine + j, 8)
                send_to(i, out_of(i), into.at[mine], send_sem, recv_sem)
                return carry

            lax.fori_loop(1 if k == 0 else 0, 8, one, 0)
        pltpu.make_async_copy(out_of(mine), into.at[mine], recv_sem).start()

    def wait_bytes(ref, sem):
        pltpu.make_async_copy(ref, ref, sem).wait()

    scatter(lambda i: gain_out.at[i // 8], gain_in, send_sems.at[0], gain_sems.at[plane_of_me])
    scatter(lambda i: bwd_out.at[i], bwd_in, send_sems.at[1], bwd_sems.at[plane_of_me])
    scatter(lambda i: fwd_out.at[i], fwd_in, send_sems.at[2], fwd_sems.at[plane_of_me])

    @pl.when(jnp.logical_not(early))
    def _():
        pl.semaphore_signal(ready, inc=1, device_id={"head": core}, device_id_type=MESH)

    def exchange(src, dst, send_sem, recv_sem):
        copy = pltpu.make_async_remote_copy(
            src_ref=src, dst_ref=dst, send_sem=send_sem, recv_sem=recv_sem,
            device_id=other_half, device_id_type=MESH,
        )
        copy.start()
        return copy

    copies = []
    for k in (0, 1, 3, 2):
        plane = lax.rem(plane_of_me + k, 4)
        sources = pl.ds(plane * 8, 8)
        at = pl.ds(plane * 4, 4)
        wait_bytes(gain_in.at[sources], gain_sems.at[plane])
        wait_bytes(bwd_in.at[sources], bwd_sems.at[plane])
        for j in range(4):
            l = plane * 4 + j
            gain_tot[l] = gain_in[2 * l] * gain_in[2 * l + 1]
            bwd_tot[l] = bwd_in[2 * l] + gain_in[2 * l] * bwd_in[2 * l + 1]
        exchange(gain_tot.at[at], gain_oth.at[at], send_sems.at[3], mid_gain_sems.at[plane])
        exchange(bwd_tot.at[at], bwd_oth.at[at], mid_bwd_sems.at[0, plane], mid_bwd_sems.at[1, plane])
    fwd_copies = []
    for plane in range(4):
        wait_bytes(fwd_in.at[plane * 8 : plane * 8 + 8], fwd_sems.at[plane])
        for l in range(plane * 4, plane * 4 + 4):
            fwd_tot[l] = fwd_in[2 * l] * gain_in[2 * l + 1] + fwd_in[2 * l + 1]
        at = slice(plane * 4, plane * 4 + 4)
        fwd_copies.append(exchange(fwd_tot.at[at], fwd_oth.at[at], mid_fwd_sems.at[0, plane], mid_fwd_sems.at[1, plane]))

    row = lax.broadcasted_iota(jnp.int32, (Q, Q), 0)
    col = lax.broadcasted_iota(jnp.int32, (Q, Q), 1)
    later = col >= row
    inner = dot(b_blk, c_blk, NT)
    pairs = jnp.zeros((Q, Q), jnp.float32)
    for block in range(BLOCKS):
        at = slice(block * 128, block * 128 + 128)
        x_blk = x_ref[:, at]
        dy_blk = dy_ref[:, at]
        parts = []
        for side in range(2):
            h = 2 * block + side
            diff = cum[h : h + 1, :] - columns[:, h : h + 1]
            weights = jnp.exp(jnp.where(later, diff, -1e30))
            x_side = jnp.where(first_lanes == (side == 0), x_blk, jnp.zeros_like(x_blk))
            pairs = pairs + dot(x_side, dy_blk, NT) * weights
            scores = (inner * weights).astype(jnp.bfloat16)
            parts.append(dot(scores, dy_blk, NN))
        local_x[:, at] = jnp.where(first_lanes, parts[0], parts[1])
    local_b[...] = dot(pairs.astype(jnp.bfloat16), c_blk, NN)
    local_c[...] = dot(jnp.transpose(pairs).astype(jnp.bfloat16), b_blk, NN)

    def send_back(out, into, plane, n):
        def one(k, carry):
            i = plane * 8 + lax.rem(mine + k, 8)

            @pl.when(i != mine)
            def _():
                send_to(i, out.at[i], into.at[mine], send_sems.at[n], recv_sems.at[n])

            @pl.when(i == mine)
            def _():
                pltpu.make_async_copy(out.at[mine], into.at[mine], recv_sems.at[n]).start()

            return carry

        lax.fori_loop(0, 8, one, 0)

    def send_all(out, into, n):
        def one(k, carry):
            i = lax.rem(mine + 13 * k, GROUP)
            send_to(i, out.at[i], into.at[mine], send_sems.at[n], recv_sems.at[n])
            return carry

        lax.fori_loop(1, GROUP, one, 0)
        pltpu.make_async_copy(out.at[mine], into.at[mine], recv_sems.at[n]).start()

    is_left = jnp.full((ROWS, 128), half) == 0
    cur = jnp.zeros((ROWS, 128), jnp.float32)
    for plane in reversed(range(4)):
        at = slice(plane * 4, plane * 4 + 4)
        wait_bytes(gain_oth.at[at], mid_gain_sems.at[plane])
        wait_bytes(bwd_oth.at[at], mid_bwd_sems.at[1, plane])
        for l in reversed(range(plane * 4, plane * 4 + 4)):
            cur = jnp.where(is_left, bwd_oth[l] + gain_oth[l] * cur, cur)
            leave_out[2 * l + 1] = cur
            cur = bwd_in[2 * l + 1] + gain_in[2 * l + 1] * cur
            leave_out[2 * l] = cur
            cur = bwd_in[2 * l] + gain_in[2 * l] * cur
            cur = jnp.where(is_left, cur, bwd_oth[l] + gain_oth[l] * cur)
        send_back(leave_out, leave_in, plane, 4)

    @pl.when(early)
    def _():
        pl.semaphore_wait(ready, 3)
        tell_later(ready)

    cur = jnp.zeros((ROWS, 128), jnp.float32)
    for plane in range(4):
        fwd_copies[plane].wait_recv()
        for l in range(plane * 4, plane * 4 + 4):
            cur = jnp.where(is_left, cur, fwd_oth[l] + gain_oth[l] * cur)
            enter_out[2 * l] = cur
            cur = fwd_in[2 * l] + gain_in[2 * l] * cur
            enter_out[2 * l + 1] = cur
            cur = fwd_in[2 * l + 1] + gain_in[2 * l + 1] * cur
            cur = jnp.where(is_left, fwd_oth[l] + gain_oth[l] * cur, cur)
    send_all(enter_out, enter_in, 5)

    def core_exchange(n, part, at):
        copy = pltpu.make_async_remote_copy(
            src_ref=core_out.at[n, at, 1 - core], dst_ref=core_in.at[n, at], send_sem=core_sems.at[0, n, part],
            recv_sem=core_sems.at[1, n, part], device_id=other_core, device_id_type=MESH,
        )
        copy.start()
        return copy

    def send_part(n, to):
        slot = z_hi - (z_hi > to).astype(jnp.int32)
        pltpu.make_async_remote_copy(
            src_ref=part_out.at[n, to], dst_ref=part_in.at[n, slot],
            send_sem=part_send.at[n], recv_sem=part_recv.at[n],
            device_id={"head": to * 2 + core}, device_id_type=MESH,
        ).start()

    def sum_heads(n, local, scaled_ref, state_in):
        states = [
            state_in[block * 8 : block * 8 + 8].reshape(STATE, 128).astype(jnp.bfloat16)
            for block in range(BLOCKS)
        ]
        pieces = (slice(0, 1), slice(1, 4))
        exchanges = []
        for part, at in enumerate(pieces):
            rows = slice(at.start * 2 * PART, at.stop * 2 * PART)
            total = local[rows]
            for block in range(BLOCKS):
                total = total + dot(scaled_ref[rows, block * 128 : block * 128 + 128], states[block], NT)
            core_out[n, at] = total.reshape(at.stop - at.start, 2, PART, 128)
            exchanges.append(core_exchange(n, part, at))
        if n == 0:
            @pl.when(jnp.logical_not(early))
            def _():
                pl.semaphore_wait(ready, 1)

        for part, at in enumerate(pieces):
            exchanges[part].wait_recv()
            part_out[n, at] = core_out[n, at, core] + core_in[n, at]
            for to in range(at.start, at.stop):
                @pl.when(z_hi != to)
                def _(to=to):
                    send_part(n, to)

        copies.extend(exchanges)
        return states

    wait_bytes(leave_in, recv_sems.at[4])
    leaves = sum_heads(0, local_b, xs_ref, leave_in)
    for block in range(BLOCKS):
        at = slice(block * 128, block * 128 + 128)
        gx_ref[:, at] = (local_x[:, at] + end_ref[:, at] * dot(b_blk, leaves[block], NN)).astype(jnp.bfloat16)
    stores = [pltpu.make_async_copy(gx_ref, gx_hbm, out_sems.at[0])]
    stores[0].start()

    wait_bytes(enter_in, recv_sems.at[5])
    sum_heads(1, local_c, ys_ref, enter_in)

    wait_bytes(gain_in.at[pl.ds(0, GROUP - 1)], send_sems.at[0])
    wait_bytes(gain_oth, send_sems.at[3])
    for n, ref in ((1, bwd_in), (2, fwd_in), (4, leave_in), (5, enter_in)):
        wait_bytes(ref.at[pl.ds(0, GROUP - 1)], send_sems.at[n])
    for plane in range(4):
        at = slice(plane * 4, plane * 4 + 4)
        wait_bytes(bwd_tot.at[at], mid_bwd_sems.at[0, plane])
        fwd_copies[plane].wait_send()

    for n, (out, out_hbm) in enumerate(((gb_ref, gb_hbm), (gc_ref, gc_hbm))):
        wait_bytes(part_in.at[n], part_recv.at[n])
        out[...] = part_out[n, z_hi] + part_in[n, 0] + part_in[n, 1] + part_in[n, 2]
        stores.append(pltpu.make_async_copy(out, out_hbm, out_sems.at[1 + n]))
        stores[-1].start()
    for n in range(2):
        wait_bytes(part_in.at[n], part_send.at[n])
        for part in range(2):
            copies[2 * n + part].wait_send()
    for store in stores:
        store.wait()


def place(gx_in, gb_in, gc_in, gx_out, gb_out, gc_out, gx_buf, gb_buf, gc_buf, in_sems, out_sems):
    rows = Q // PIECES
    parts = [(gx_in.at[at], gx_buf.at[at], gx_out.at[at]) for at in (pl.ds(n * rows, rows) for n in range(PIECES))]
    parts += [(gb_in, gb_buf, gb_out), (gc_in, gc_buf, gc_out)]
    loads = [pltpu.make_async_copy(src, buf, in_sems.at[n]) for n, (src, buf, dst) in enumerate(parts)]
    stores = [pltpu.make_async_copy(buf, dst, out_sems.at[n]) for n, (src, buf, dst) in enumerate(parts)]
    for load in loads:
        load.start()
    for load, store in zip(loads, stores):
        load.wait()
        store.start()
    for store in stores:
        store.wait()


def on_device(x_seq, grad_out, b_proj, c_proj, decay_rate):
    def vmem(shape, dtype=jnp.float32):
        return pltpu.VMEM(shape, dtype)

    def dma(*shape):
        return pltpu.SemaphoreType.DMA(shape)

    chunks = (GROUP, ROWS, 128)
    totals = (LINES, ROWS, 128)
    wide = (Q, HEADS * WIDTH)
    hbm = pl.BlockSpec(memory_space=pltpu.HBM)
    results = (
        jax.ShapeDtypeStruct(wide, jnp.bfloat16),
        jax.ShapeDtypeStruct((PART, STATE), jnp.float32),
        jax.ShapeDtypeStruct((PART, STATE), jnp.float32),
    )
    sums = pl.pallas_call(
        kernel,
        out_shape=results,
        in_specs=[hbm] * 5,
        out_specs=(hbm,) * 3,
        scratch_shapes=[
            vmem(wide, jnp.bfloat16), vmem(wide, jnp.bfloat16),
            vmem((Q, STATE), jnp.bfloat16), vmem((Q, STATE), jnp.bfloat16), vmem((HEADS, Q)),
            vmem(wide, jnp.bfloat16), vmem((PART, STATE)), vmem((PART, STATE)),
            vmem(chunks), vmem(chunks), vmem((BLOCKS, 1, 128)),
            vmem(chunks), vmem(chunks), vmem((GROUP, 1, 128)),
            vmem(totals), vmem(totals), vmem((LINES, 1, 128)),
            vmem(totals), vmem(totals), vmem((LINES, 1, 128)),
            vmem(chunks), vmem(chunks), vmem(chunks), vmem(chunks),
            vmem(wide, jnp.bfloat16), vmem(wide, jnp.bfloat16),
            vmem(wide), vmem(wide),
            vmem((Q, STATE)), vmem((Q, STATE)),
            vmem((2, 4, 2, PART, 128)), vmem((2, 4, PART, 128)),
            vmem((2, 4, PART, 128)), vmem((2, 3, PART, 128)),
            dma(5), dma(6), dma(6), dma(4), dma(4), dma(2, 4), dma(2, 4), dma(4),
            dma(4), dma(2, 2, 2), dma(2), dma(2), dma(3), pltpu.SemaphoreType.REGULAR,
        ],
        compiler_params=pltpu.CompilerParams(
            collective_id=0, has_side_effects=True, vmem_limit_bytes=56 << 20
        ),
    )(x_seq, grad_out, b_proj, c_proj, decay_rate)
    return pl.pallas_call(
        place,
        out_shape=results,
        in_specs=[hbm] * 3,
        out_specs=(hbm,) * 3,
        scratch_shapes=[
            vmem(wide, jnp.bfloat16), vmem((PART, STATE)), vmem((PART, STATE)),
            dma(PIECES + 2), dma(PIECES + 2),
        ],
        compiler_params=pltpu.CompilerParams(vmem_limit_bytes=56 << 20),
    )(*sums)


def solution(mesh):
    placed = (P("ctx", "head"), P("ctx", "head"), P("ctx", None), P("ctx", None), P("head", "ctx"))
    return jax.shard_map(
        on_device,
        mesh=mesh,
        in_specs=placed,
        out_specs=(P("ctx", "head"), P(("ctx", "head"), None), P(("ctx", "head"), None)),
        check_vma=False,
    )
```

time: 59.9 us -> 53.8 us (0.90)
  local copies, waits for them, and re-layouts: 6.18 us -> 0 us
    unnamed x13 -> x0, local copies, waits for them, and re-layouts: 6.18 us -> none
    pallas_call x1 -> x2, Pallas kernels: 52.8 us -> 53 us  [the longest x1 51.3 us: on_device(): pl.pallas_call(kernel, out_shape=results, in_specs=[hbm] * 5, out_specs=(...]
where the time goes in v2:
time: 53.8 us; the launch traced here: 53.6 us
  Pallas kernels  53 us (99%)
  between operations  0.64 us (1%)
    pallas_call x1, Pallas kernels, on_device(): pl.pallas_call(kernel, out_shape=results, in_specs=[hbm] * 5, out_specs=(...  51.3 us
    pallas_call x1, Pallas kernels, on_device(): pl.pallas_call(place, out_shape=results, in_specs=[hbm] * 3, out_specs=(h...  1.67 us

profile of v2, /device:TPU:32, one launch (start us, length us, event | category | flops | bytes accessed | tf_op | source)
XLA Modules:
  0.0 53.6 jit_solution(15481462942580487145)
XLA Ops:
  0.6 51.3 %shard_map.76 = (bf16[256,512]{1,0:T(8,128)(2,1)}, f32[32,128]{1,0:T(8,128)}, f32[32,128]{1,0:T(8,128)}) custom-call(bf16[256,512]{1,0:T(8,128)(2,1)} %x_hbm.1, bf16[256,512]{1,0:T(8,128)(2,1)} %dy_hbm.1, bf16[256,128]{1,0:T(8,128)(2,1)} %b_hbm.1, bf16[256,128]{1,0:T(8,128)(2,1)} %c_hbm.1, f32[8,256]{1,0:T(8,128)} %decay_hbm.1), custom_call_target="tpu_custom_call" | custom-call | tf_op jit(solution)/shard_map/pallas_call | solution.py:366
  51.9 1.7 %shard_map.77 = (bf16[256,512]{1,0:T(8,128)(2,1)}, f32[32,128]{1,0:T(8,128)}, f32[32,128]{1,0:T(8,128)}) custom-call(bf16[256,512]{1,0:T(8,128)(2,1)} %get-tuple-element.6.gx_in, f32[32,128]{1,0:T(8,128)} %get-tuple-element.7.gb_in, f32[32,128]{1,0:T(8,128)} %get-tuple-element.8.gc_in), custom_call_target="tpu_custom_call" | custom-call | tf_op jit(solution)/shard_map/pallas_call | solution.py:392

commit v3 on v2

--- a/solution.py
+++ b/solution.py
@@ -14,6 +14,7 @@
 GROUP = 32
 ROWS = 16
 LINES = 16
+HALF = 8
 PART = 32
 PIECES = 4
 
@@ -30,13 +31,13 @@
     x_hbm, dy_hbm, b_hbm, c_hbm, decay_hbm,
     gx_hbm, gb_hbm, gc_hbm,
     x_ref, dy_ref, b_ref, c_ref, decay_ref, gx_ref, gb_ref, gc_ref,
-    fwd_out, bwd_out, gain_out, fwd_in, bwd_in, gain_in,
-    fwd_tot, bwd_tot, gain_tot, fwd_oth, bwd_oth, gain_oth,
+    fwd_out, bwd_out, fwd_in, bwd_in,
+    fwd_tot, bwd_tot, fwd_oth, bwd_oth,
     enter_out, leave_out, enter_in, leave_in,
     xs_ref, ys_ref, end_ref, local_x, local_b, local_c,
     core_out, core_in, part_out, part_in,
-    in_sems, send_sems, recv_sems, fwd_sems, bwd_sems, mid_fwd_sems, mid_bwd_sems, mid_gain_sems,
-    gain_sems, core_sems, part_send, part_recv, out_sems, ready,
+    in_sems, send_sems, recv_sems, fwd_sems, bwd_sems, mid_fwd_sems, mid_bwd_sems,
+    core_sems, part_send, part_recv, out_sems, ready,
 ):
     me = lax.axis_index("ctx")
     head = lax.axis_index("head")
@@ -110,11 +111,15 @@
         ys = (dy_ref[:, at].astype(jnp.float32) * start_blk).astype(jnp.bfloat16)
         xs_ref[:, at] = xs
         ys_ref[:, at] = ys
-        gain_out[block] = start_blk[Q - 1 : Q, :]
-        bwd_out[block * 8 : block * 8 + 8] = dot(c_blk, ys, TN).reshape(8, ROWS, 128)
+        bwd_out[block * 8 : block * 8 + 8, ROWS:] = jnp.broadcast_to(start_blk[Q - 1 : Q, :][None], (8, 1, 128))
+        bwd_out[block * 8 : block * 8 + 8, :ROWS] = dot(c_blk, ys, TN).reshape(8, ROWS, 128)
         fwd_out[block * 8 : block * 8 + 8] = dot(b_blk, xs, TN).reshape(8, ROWS, 128)
 
     pl.semaphore_wait(barrier, GROUP - 1 + 1 + 1 + jnp.where(early, 0, 1))
+
+    @pl.when(jnp.logical_not(early))
+    def _():
+        pl.semaphore_signal(ready, inc=1, device_id={"head": core}, device_id_type=MESH)
 
     def send_to(i, src, dst, send_sem, recv_sem):
         pltpu.make_async_remote_copy(
@@ -137,13 +142,8 @@
     def wait_bytes(ref, sem):
         pltpu.make_async_copy(ref, ref, sem).wait()
 
-    scatter(lambda i: gain_out.at[i // 8], gain_in, send_sems.at[0], gain_sems.at[plane_of_me])
     scatter(lambda i: bwd_out.at[i], bwd_in, send_sems.at[1], bwd_sems.at[plane_of_me])
     scatter(lambda i: fwd_out.at[i], fwd_in, send_sems.at[2], fwd_sems.at[plane_of_me])
-
-    @pl.when(jnp.logical_not(early))
-    def _():
-        pl.semaphore_signal(ready, inc=1, device_id={"head": core}, device_id_type=MESH)
 
     def exchange(src, dst, send_sem, recv_sem):
         copy = pltpu.make_async_remote_copy(
@@ -154,25 +154,33 @@
         return copy
 
     copies = []
+    def gain_of(j):
+        return bwd_in[j, ROWS:]
+
+    def other_gain(l):
+        return bwd_oth[l, ROWS:]
+
     for k in (0, 1, 3, 2):
         plane = lax.rem(plane_of_me + k, 4)
         sources = pl.ds(plane * 8, 8)
         at = pl.ds(plane * 4, 4)
-        wait_bytes(gain_in.at[sources], gain_sems.at[plane])
         wait_bytes(bwd_in.at[sources], bwd_sems.at[plane])
         for j in range(4):
             l = plane * 4 + j
-            gain_tot[l] = gain_in[2 * l] * gain_in[2 * l + 1]
-            bwd_tot[l] = bwd_in[2 * l] + gain_in[2 * l] * bwd_in[2 * l + 1]
-        exchange(gain_tot.at[at], gain_oth.at[at], send_sems.at[3], mid_gain_sems.at[plane])
+            first_gain = gain_of(2 * l)
+            bwd_tot[l, :ROWS] = bwd_in[2 * l, :ROWS] + first_gain * bwd_in[2 * l + 1, :ROWS]
+            bwd_tot[l, ROWS:] = first_gain * gain_of(2 * l + 1)
         exchange(bwd_tot.at[at], bwd_oth.at[at], mid_bwd_sems.at[0, plane], mid_bwd_sems.at[1, plane])
-    fwd_copies = []
     for plane in range(4):
         wait_bytes(fwd_in.at[plane * 8 : plane * 8 + 8], fwd_sems.at[plane])
-        for l in range(plane * 4, plane * 4 + 4):
-            fwd_tot[l] = fwd_in[2 * l] * gain_in[2 * l + 1] + fwd_in[2 * l + 1]
-        at = slice(plane * 4, plane * 4 + 4)
-        fwd_copies.append(exchange(fwd_tot.at[at], fwd_oth.at[at], mid_fwd_sems.at[0, plane], mid_fwd_sems.at[1, plane]))
+    fwd_copies = []
+    for part in range(2):
+        at = slice(part * HALF, part * HALF + HALF)
+        for l in range(LINES):
+            fwd_tot[part, l] = fwd_in[2 * l, at] * gain_of(2 * l + 1) + fwd_in[2 * l + 1, at]
+        fwd_copies.append(
+            exchange(fwd_tot.at[part], fwd_oth.at[part], mid_fwd_sems.at[0, part], mid_fwd_sems.at[1, part])
+        )
 
     row = lax.broadcasted_iota(jnp.int32, (Q, Q), 0)
     col = lax.broadcasted_iota(jnp.int32, (Q, Q), 1)
@@ -212,28 +220,29 @@
 
         lax.fori_loop(0, 8, one, 0)
 
-    def send_all(out, into, n):
+    def send_all(out, into, at, n):
+        slot = into.at[mine, at]
+
         def one(k, carry):
             i = lax.rem(mine + 13 * k, GROUP)
-            send_to(i, out.at[i], into.at[mine], send_sems.at[n], recv_sems.at[n])
+            send_to(i, out.at[i], slot, send_sems.at[n], recv_sems.at[n])
             return carry
 
         lax.fori_loop(1, GROUP, one, 0)
-        pltpu.make_async_copy(out.at[mine], into.at[mine], recv_sems.at[n]).start()
+        pltpu.make_async_copy(out.at[mine], slot, recv_sems.at[n]).start()
 
     is_left = jnp.full((ROWS, 128), half) == 0
     cur = jnp.zeros((ROWS, 128), jnp.float32)
     for plane in reversed(range(4)):
         at = slice(plane * 4, plane * 4 + 4)
-        wait_bytes(gain_oth.at[at], mid_gain_sems.at[plane])
         wait_bytes(bwd_oth.at[at], mid_bwd_sems.at[1, plane])
         for l in reversed(range(plane * 4, plane * 4 + 4)):
-            cur = jnp.where(is_left, bwd_oth[l] + gain_oth[l] * cur, cur)
+            cur = jnp.where(is_left, bwd_oth[l, :ROWS] + other_gain(l) * cur, cur)
             leave_out[2 * l + 1] = cur
-            cur = bwd_in[2 * l + 1] + gain_in[2 * l + 1] * cur
+            cur = bwd_in[2 * l + 1, :ROWS] + gain_of(2 * l + 1) * cur
             leave_out[2 * l] = cur
-            cur = bwd_in[2 * l] + gain_in[2 * l] * cur
-            cur = jnp.where(is_left, cur, bwd_oth[l] + gain_oth[l] * cur)
+            cur = bwd_in[2 * l, :ROWS] + gain_of(2 * l) * cur
+            cur = jnp.where(is_left, cur, bwd_oth[l, :ROWS] + other_gain(l) * cur)
         send_back(leave_out, leave_in, plane, 4)
 
     @pl.when(early)
@@ -241,17 +250,19 @@
         pl.semaphore_wait(ready, 3)
         tell_later(ready)
 
-    cur = jnp.zeros((ROWS, 128), jnp.float32)
-    for plane in range(4):
-        fwd_copies[plane].wait_recv()
-        for l in range(plane * 4, plane * 4 + 4):
-            cur = jnp.where(is_left, cur, fwd_oth[l] + gain_oth[l] * cur)
-            enter_out[2 * l] = cur
-            cur = fwd_in[2 * l] + gain_in[2 * l] * cur
-            enter_out[2 * l + 1] = cur
-            cur = fwd_in[2 * l + 1] + gain_in[2 * l + 1] * cur
-            cur = jnp.where(is_left, fwd_oth[l] + gain_oth[l] * cur, cur)
-    send_all(enter_out, enter_in, 5)
+    for part in range(2):
+        at = slice(part * HALF, part * HALF + HALF)
+        left = is_left[at]
+        cur = jnp.zeros((HALF, 128), jnp.float32)
+        fwd_copies[part].wait_recv()
+        for l in range(LINES):
+            cur = jnp.where(left, cur, fwd_oth[part, l] + other_gain(l) * cur)
+            enter_out[part, 2 * l] = cur
+            cur = fwd_in[2 * l, at] + gain_of(2 * l) * cur
+            enter_out[part, 2 * l + 1] = cur
+            cur = fwd_in[2 * l + 1, at] + gain_of(2 * l + 1) * cur
+            cur = jnp.where(left, fwd_oth[part, l] + other_gain(l) * cur, cur)
+        send_all(enter_out.at[part], enter_in, at, 5)
 
     def core_exchange(n, part, at):
         copy = pltpu.make_async_remote_copy(
@@ -284,43 +295,58 @@
             core_out[n, at] = total.reshape(at.stop - at.start, 2, PART, 128)
             exchanges.append(core_exchange(n, part, at))
         if n == 0:
-            @pl.when(jnp.logical_not(early))
-            def _():
-                pl.semaphore_wait(ready, 1)
-
+            for block in range(BLOCKS):
+                at = slice(block * 128, block * 128 + 128)
+                carried = end_ref[:, at] * dot(b_blk, states[block], NN)
+                gx_ref[:, at] = (local_x[:, at] + carried).astype(jnp.bfloat16)
         for part, at in enumerate(pieces):
             exchanges[part].wait_recv()
             part_out[n, at] = core_out[n, at, core] + core_in[n, at]
-            for to in range(at.start, at.stop):
-                @pl.when(z_hi != to)
-                def _(to=to):
-                    send_part(n, to)
+            if part == 0:
+                @pl.when(jnp.logical_not(early))
+                def _():
+                    send_part(n, 0)
 
         copies.extend(exchanges)
-        return states
 
     wait_bytes(leave_in, recv_sems.at[4])
-    leaves = sum_heads(0, local_b, xs_ref, leave_in)
-    for block in range(BLOCKS):
-        at = slice(block * 128, block * 128 + 128)
-        gx_ref[:, at] = (local_x[:, at] + end_ref[:, at] * dot(b_blk, leaves[block], NN)).astype(jnp.bfloat16)
+    sum_heads(0, local_b, xs_ref, leave_in)
     stores = [pltpu.make_async_copy(gx_ref, gx_hbm, out_sems.at[0])]
     stores[0].start()
 
     wait_bytes(enter_in, recv_sems.at[5])
     sum_heads(1, local_c, ys_ref, enter_in)
 
-    wait_bytes(gain_in.at[pl.ds(0, GROUP - 1)], send_sems.at[0])
-    wait_bytes(gain_oth, send_sems.at[3])
+    @pl.when(early)
+    def _():
+        wait_bytes(part_in.at[0], part_recv.at[0])
+
+    @pl.when(jnp.logical_not(early))
+    def _():
+        pl.semaphore_wait(ready, 1)
+
+    for n in range(2):
+        for to in range(1, 4):
+            @pl.when(z_hi != to)
+            def _(n=n, to=to):
+                send_part(n, to)
+
+    @pl.when(jnp.logical_not(early))
+    def _():
+        wait_bytes(part_in.at[0], part_recv.at[0])
+
+
     for n, ref in ((1, bwd_in), (2, fwd_in), (4, leave_in), (5, enter_in)):
         wait_bytes(ref.at[pl.ds(0, GROUP - 1)], send_sems.at[n])
     for plane in range(4):
         at = slice(plane * 4, plane * 4 + 4)
         wait_bytes(bwd_tot.at[at], mid_bwd_sems.at[0, plane])
-        fwd_copies[plane].wait_send()
+    for copy in fwd_copies:
+        copy.wait_send()
 
     for n, (out, out_hbm) in enumerate(((gb_ref, gb_hbm), (gc_ref, gc_hbm))):
-        wait_bytes(part_in.at[n], part_recv.at[n])
+        if n == 1:
+            wait_bytes(part_in.at[1], part_recv.at[1])
         out[...] = part_out[n, z_hi] + part_in[n, 0] + part_in[n, 1] + part_in[n, 2]
         stores.append(pltpu.make_async_copy(out, out_hbm, out_sems.at[1 + n]))
         stores[-1].start()
@@ -355,7 +381,8 @@
         return pltpu.SemaphoreType.DMA(shape)
 
     chunks = (GROUP, ROWS, 128)
-    totals = (LINES, ROWS, 128)
+    totals = (2, LINES, HALF, 128)
+    returns = (2, GROUP, HALF, 128)
     wide = (Q, HEADS * WIDTH)
     hbm = pl.BlockSpec(memory_space=pltpu.HBM)
     results = (
@@ -372,18 +399,16 @@
             vmem(wide, jnp.bfloat16), vmem(wide, jnp.bfloat16),
             vmem((Q, STATE), jnp.bfloat16), vmem((Q, STATE), jnp.bfloat16), vmem((HEADS, Q)),
             vmem(wide, jnp.bfloat16), vmem((PART, STATE)), vmem((PART, STATE)),
-            vmem(chunks), vmem(chunks), vmem((BLOCKS, 1, 128)),
-            vmem(chunks), vmem(chunks), vmem((GROUP, 1, 128)),
-            vmem(totals), vmem(totals), vmem((LINES, 1, 128)),
-            vmem(totals), vmem(totals), vmem((LINES, 1, 128)),
-            vmem(chunks), vmem(chunks), vmem(chunks), vmem(chunks),
+            vmem(chunks), vmem((GROUP, ROWS + 1, 128)), vmem(chunks), vmem((GROUP, ROWS + 1, 128)),
+            vmem(totals), vmem((LINES, ROWS + 1, 128)), vmem(totals), vmem((LINES, ROWS + 1, 128)),
+            vmem(returns), vmem(chunks), vmem(chunks), vmem(chunks),
             vmem(wide, jnp.bfloat16), vmem(wide, jnp.bfloat16),
             vmem(wide), vmem(wide),
             vmem((Q, STATE)), vmem((Q, STATE)),
             vmem((2, 4, 2, PART, 128)), vmem((2, 4, PART, 128)),
             vmem((2, 4, PART, 128)), vmem((2, 3, PART, 128)),
-            dma(5), dma(6), dma(6), dma(4), dma(4), dma(2, 4), dma(2, 4), dma(4),
-            dma(4), dma(2, 2, 2), dma(2), dma(2), dma(3), pltpu.SemaphoreType.REGULAR,
+            dma(5), dma(6), dma(6), dma(4), dma(4), dma(2, 2), dma(2, 4),
+            dma(2, 2, 2), dma(2), dma(2), dma(3), pltpu.SemaphoreType.REGULAR,
         ],
         compiler_params=pltpu.CompilerParams(
             collective_id=0, has_side_effects=True, vmem_limit_bytes=56 << 20

time: 53.8 us -> 52 us (0.967)
  the two profiles are of different devices: /device:TPU:32 before, /device:TPU:1 now
where the time goes in v3:
time: 52 us; the launch traced here: 51.1 us
  Pallas kernels  50.4 us (97%)
  between operations  0.64 us (1%)
    pallas_call x1, Pallas kernels, on_device(): pl.pallas_call(kernel, out_shape=results, in_specs=[hbm] * 5, out_specs=(...  48.7 us
    pallas_call x1, Pallas kernels, on_device(): pl.pallas_call(place, out_shape=results, in_specs=[hbm] * 3, out_specs=(h...  1.67 us

profile of v3, /device:TPU:1, one launch (start us, length us, event | category | flops | bytes accessed | tf_op | source)
XLA Modules:
  0.0 51.1 jit_solution(13306116556341958309)
XLA Ops:
  0.6 48.7 %shard_map.76 = (bf16[256,512]{1,0:T(8,128)(2,1)}, f32[32,128]{1,0:T(8,128)}, f32[32,128]{1,0:T(8,128)}) custom-call(bf16[256,512]{1,0:T(8,128)(2,1)} %x_hbm.1, bf16[256,512]{1,0:T(8,128)(2,1)} %dy_hbm.1, bf16[256,128]{1,0:T(8,128)(2,1)} %b_hbm.1, bf16[256,128]{1,0:T(8,128)(2,1)} %c_hbm.1, f32[8,256]{1,0:T(8,128)} %decay_hbm.1), custom_call_target="tpu_custom_call" | custom-call | tf_op jit(solution)/shard_map/pallas_call | solution.py:393
  49.4 1.7 %shard_map.77 = (bf16[256,512]{1,0:T(8,128)(2,1)}, f32[32,128]{1,0:T(8,128)}, f32[32,128]{1,0:T(8,128)}) custom-call(bf16[256,512]{1,0:T(8,128)(2,1)} %get-tuple-element.6.gx_in, f32[32,128]{1,0:T(8,128)} %get-tuple-element.7.gb_in, f32[32,128]{1,0:T(8,128)} %get-tuple-element.8.gc_in), custom_call_target="tpu_custom_call" | custom-call | tf_op jit(solution)/shard_map/pallas_call | solution.py:417

commit v4 on v3

--- a/solution.py
+++ b/solution.py
@@ -66,11 +66,11 @@
 
     def greet(k, carry):
         pl.semaphore_signal(
-            barrier, inc=1, device_id={"ctx": ctx_of(lax.rem(mine + k, GROUP))}, device_id_type=MESH
+            barrier, inc=1, device_id={"ctx": ctx_of(lax.rem(mine + 13 * k, GROUP))}, device_id_type=MESH
         )
         return carry
 
-    lax.fori_loop(1, GROUP, greet, 0)
+    lax.fori_loop(1, GROUP, greet, 0, unroll=True)
     pl.semaphore_signal(barrier, inc=1, device_id=other_half, device_id_type=MESH)
     pl.semaphore_signal(barrier, inc=1, device_id=other_core, device_id_type=MESH)
     def tell_later(sem):
@@ -136,7 +136,7 @@
                 send_to(i, out_of(i), into.at[mine], send_sem, recv_sem)
                 return carry
 
-            lax.fori_loop(1 if k == 0 else 0, 8, one, 0)
+            lax.fori_loop(1 if k == 0 else 0, 8, one, 0, unroll=True)
         pltpu.make_async_copy(out_of(mine), into.at[mine], recv_sem).start()
 
     def wait_bytes(ref, sem):
@@ -228,7 +228,7 @@
             send_to(i, out.at[i], slot, send_sems.at[n], recv_sems.at[n])
             return carry
 
-        lax.fori_loop(1, GROUP, one, 0)
+        lax.fori_loop(1, GROUP, one, 0, unroll=True)
         pltpu.make_async_copy(out.at[mine], slot, recv_sems.at[n]).start()
 
     is_left = jnp.full((ROWS, 128), half) == 0
@@ -294,32 +294,33 @@
                 total = total + dot(scaled_ref[rows, block * 128 : block * 128 + 128], states[block], NT)
             core_out[n, at] = total.reshape(at.stop - at.start, 2, PART, 128)
             exchanges.append(core_exchange(n, part, at))
-        if n == 0:
-            for block in range(BLOCKS):
-                at = slice(block * 128, block * 128 + 128)
-                carried = end_ref[:, at] * dot(b_blk, states[block], NN)
-                gx_ref[:, at] = (local_x[:, at] + carried).astype(jnp.bfloat16)
-        for part, at in enumerate(pieces):
+        def settle(part):
+            at = pieces[part]
             exchanges[part].wait_recv()
             part_out[n, at] = core_out[n, at, core] + core_in[n, at]
-            if part == 0:
-                @pl.when(jnp.logical_not(early))
-                def _():
-                    send_part(n, 0)
-
+
+        settle(0)
+
+        @pl.when(jnp.logical_not(early))
+        def _():
+            send_part(n, 0)
+
+        later_sums.append(settle)
         copies.extend(exchanges)
 
     wait_bytes(leave_in, recv_sems.at[4])
+    later_sums = []
     sum_heads(0, local_b, xs_ref, leave_in)
+    wait_bytes(enter_in, recv_sems.at[5])
+    sum_heads(1, local_c, ys_ref, enter_in)
+    for block in range(BLOCKS):
+        at = slice(block * 128, block * 128 + 128)
+        leave = leave_in[block * 8 : block * 8 + 8].reshape(STATE, 128).astype(jnp.bfloat16)
+        gx_ref[:, at] = (local_x[:, at] + end_ref[:, at] * dot(b_blk, leave, NN)).astype(jnp.bfloat16)
     stores = [pltpu.make_async_copy(gx_ref, gx_hbm, out_sems.at[0])]
     stores[0].start()
-
-    wait_bytes(enter_in, recv_sems.at[5])
-    sum_heads(1, local_c, ys_ref, enter_in)
-
-    @pl.when(early)
-    def _():
-        wait_bytes(part_in.at[0], part_recv.at[0])
+    for settle in later_sums:
+        settle(1)
 
     @pl.when(jnp.logical_not(early))
     def _():
@@ -331,10 +332,7 @@
             def _(n=n, to=to):
                 send_part(n, to)
 
-    @pl.when(jnp.logical_not(early))
-    def _():
-        wait_bytes(part_in.at[0], part_recv.at[0])
-
+    wait_bytes(part_in.at[0], part_recv.at[0])
 
     for n, ref in ((1, bwd_in), (2, fwd_in), (4, leave_in), (5, enter_in)):
         wait_bytes(ref.at[pl.ds(0, GROUP - 1)], send_sems.at[n])

time: 52 us -> 51.2 us (0.985); the launches traced: 51.1 us -> 51 us
  no operation moved by 1% of the time
where the time goes in v4:
time: 51.2 us; the launch traced here: 51 us
  Pallas kernels  50.3 us (98%)
  between operations  0.64 us (1%)
    pallas_call x1, Pallas kernels, on_device(): pl.pallas_call(kernel, out_shape=results, in_specs=[hbm] * 5, out_specs=(...  48.7 us
    pallas_call x1, Pallas kernels, on_device(): pl.pallas_call(place, out_shape=results, in_specs=[hbm] * 3, out_specs=(h...  1.67 us

profile of v4, /device:TPU:1, one launch (start us, length us, event | category | flops | bytes accessed | tf_op | source)
XLA Modules:
  0.0 51.0 jit_solution(13780019709902315127)
XLA Ops:
  0.6 48.7 %shard_map.76 = (bf16[256,512]{1,0:T(8,128)(2,1)}, f32[32,128]{1,0:T(8,128)}, f32[32,128]{1,0:T(8,128)}) custom-call(bf16[256,512]{1,0:T(8,128)(2,1)} %x_hbm.1, bf16[256,512]{1,0:T(8,128)(2,1)} %dy_hbm.1, bf16[256,128]{1,0:T(8,128)(2,1)} %b_hbm.1, bf16[256,128]{1,0:T(8,128)(2,1)} %c_hbm.1, f32[8,256]{1,0:T(8,128)} %decay_hbm.1), custom_call_target="tpu_custom_call" | custom-call | tf_op jit(solution)/shard_map/pallas_call | solution.py:391
  49.3 1.7 %shard_map.77 = (bf16[256,512]{1,0:T(8,128)(2,1)}, f32[32,128]{1,0:T(8,128)}, f32[32,128]{1,0:T(8,128)}) custom-call(bf16[256,512]{1,0:T(8,128)(2,1)} %get-tuple-element.6.gx_in, f32[32,128]{1,0:T(8,128)} %get-tuple-element.7.gb_in, f32[32,128]{1,0:T(8,128)} %get-tuple-element.8.gc_in), custom_call_target="tpu_custom_call" | custom-call | tf_op jit(solution)/shard_map/pallas_call | solution.py:415

commit v5 on v4

--- a/solution.py
+++ b/solution.py
@@ -143,7 +143,13 @@
         pltpu.make_async_copy(ref, ref, sem).wait()
 
     scatter(lambda i: bwd_out.at[i], bwd_in, send_sems.at[1], bwd_sems.at[plane_of_me])
-    scatter(lambda i: fwd_out.at[i], fwd_in, send_sems.at[2], fwd_sems.at[plane_of_me])
+    def send_fwd(k, carry):
+        i = lax.rem(mine + 13 * k, GROUP)
+        send_to(i, fwd_out.at[i], fwd_in.at[mine], send_sems.at[2], fwd_sems.at[plane_of_me])
+        return carry
+
+    lax.fori_loop(1, GROUP, send_fwd, 0, unroll=True)
+    pltpu.make_async_copy(fwd_out.at[mine], fwd_in.at[mine], fwd_sems.at[plane_of_me]).start()
 
     def exchange(src, dst, send_sem, recv_sem):
         copy = pltpu.make_async_remote_copy(

time: 51.2 us -> 51.3 us (level)
  no operation moved by 1% of the time
where the time goes in v5:
time: 51.3 us; the launch traced here: 51.1 us
  Pallas kernels  50.5 us (98%)
  between operations  0.64 us (1%)
    pallas_call x1, Pallas kernels, on_device(): pl.pallas_call(kernel, out_shape=results, in_specs=[hbm] * 5, out_specs=(...  48.8 us
    pallas_call x1, Pallas kernels, on_device(): pl.pallas_call(place, out_shape=results, in_specs=[hbm] * 3, out_specs=(h...  1.67 us

profile of v5, /device:TPU:1, one launch (start us, length us, event | category | flops | bytes accessed | tf_op | source)
XLA Modules:
  0.0 51.1 jit_solution(1662494714832121724)
XLA Ops:
  0.6 48.8 %shard_map.76 = (bf16[256,512]{1,0:T(8,128)(2,1)}, f32[32,128]{1,0:T(8,128)}, f32[32,128]{1,0:T(8,128)}) custom-call(bf16[256,512]{1,0:T(8,128)(2,1)} %x_hbm.1, bf16[256,512]{1,0:T(8,128)(2,1)} %dy_hbm.1, bf16[256,128]{1,0:T(8,128)(2,1)} %b_hbm.1, bf16[256,128]{1,0:T(8,128)(2,1)} %c_hbm.1, f32[8,256]{1,0:T(8,128)} %decay_hbm.1), custom_call_target="tpu_custom_call" | custom-call | tf_op jit(solution)/shard_map/pallas_call | solution.py:397
  49.5 1.7 %shard_map.77 = (bf16[256,512]{1,0:T(8,128)(2,1)}, f32[32,128]{1,0:T(8,128)}, f32[32,128]{1,0:T(8,128)}) custom-call(bf16[256,512]{1,0:T(8,128)(2,1)} %get-tuple-element.6.gx_in, f32[32,128]{1,0:T(8,128)} %get-tuple-element.7.gb_in, f32[32,128]{1,0:T(8,128)} %get-tuple-element.8.gc_in), custom_call_target="tpu_custom_call" | custom-call | tf_op jit(solution)/shard_map/pallas_call | solution.py:421
